TPU v7x, 32 devices: a whole 2x2x4 slice. The times are simulated.
32 devices in a mesh: dp: 8 (over y, x, core), loop: 4 (over z).
Axes of the slice: x: 2, y: 2, z: 4, core: 2. Of those that a mesh axis runs over, the one named last changes fastest.
Arguments:
- tokens: bfloat16 [1024, 2048], P('dp', 'loop'), may hold values from -6 to 6
- norm_gain: bfloat16 [2048], replicated, may hold values from 0.25 to 1.75
- route_ids: int32 [1024, 8], P('dp'), may hold values from 0 to 127, all different within a row; in each aligned block of 128 rows (0 to 127, 128 to 255, ...) at most 16 rows name the same one
- route_weights: float32 [1024, 8], P('dp'), may hold values from 0.1 to 1
- w_gate: bfloat16 [512, 384, 2048], P(('dp', 'loop')), may hold values from -0.125 to 0.125
- w_up: bfloat16 [512, 384, 2048], P(('dp', 'loop')), may hold values from -0.125 to 0.125
- w_down: bfloat16 [512, 384, 2048], P(('dp', 'loop')), may hold values from -0.15625 to 0.15625
Outputs:
- block_out: bfloat16 [1024, 2048], P('dp', 'loop')
Inputs may be any that keep to these rules, and one draw needn't show every extreme that they name: `route_ids`: each row names 8 different experts. Within each aligned block of 128 rows no expert is named by more than 16 rows, and in some blocks an expert is named by exactly 16 rows.
All inputs are finite; a program needn't handle non-finite values.
Results may differ from a plain program's by a relative error of at most 0.0059.
Values may be sent and summed in bfloat16 or wider, within the bound.
A program may use at most 128 MiB of HBM per device.

v0:
```python
import jax
import jax.numpy as jnp
from jax import lax
from jax.sharding import PartitionSpec as P

EXPERTS = 128
HGROUPS = 4
CAP = 16


def shards(tokens, norm_gain, route_ids, route_weights, w_gate, w_up, w_down):
    row_count, slice_width = tokens.shape
    top_count = route_ids.shape[1]
    groups = lax.axis_size("dp")
    pairs_here, hidden_width, full_width = w_gate.shape
    group_experts = EXPERTS // groups
    own_experts = max(1, pairs_here // HGROUPS)
    per_expert = pairs_here // own_experts
    loop_index = lax.axis_index("loop")
    first_expert = loop_index * pairs_here // HGROUPS
    values = tokens.astype(jnp.float32)
    square_sum = lax.psum(jnp.sum(values * values, axis=1), "loop")
    row_scale = lax.rsqrt(square_sum / full_width + 1e-06)[:, None]
    gain_slice = lax.dynamic_slice_in_dim(norm_gain, loop_index * slice_width, slice_width, 0)
    normed = (values * row_scale * gain_slice.astype(jnp.float32)).astype(jnp.bfloat16)
    flat_ids = route_ids.reshape(-1)
    onehot = (flat_ids[:, None] == jnp.arange(EXPERTS, dtype=jnp.int32)[None, :]).astype(jnp.int32)
    position = jnp.sum((jnp.cumsum(onehot, axis=0) - onehot) * onehot, axis=1)
    slot_index = flat_ids * CAP + position
    pair_ids = jnp.arange(row_count * top_count, dtype=jnp.int32)
    slot_owner = (
        jnp.full((EXPERTS * CAP,), row_count, jnp.int32).at[slot_index].set(pair_ids // top_count)
    )
    owner_table = slot_owner.reshape(EXPERTS, CAP)
    local_offsets = jnp.arange(own_experts, dtype=jnp.int32)
    full_rows = lax.all_gather(normed, "loop", axis=1, tiled=True)
    padded = jnp.concatenate([full_rows, jnp.zeros((1, full_width), jnp.bfloat16)], axis=0)
    wanted = (
        jnp.arange(groups, dtype=jnp.int32)[:, None] * group_experts
        + first_expert
        + local_offsets[None, :]
    )
    send_rows = padded[owner_table[wanted]]
    arrived = lax.all_to_all(send_rows, "dp", split_axis=0, concat_axis=0, tiled=True)
    weight_shape = (own_experts, per_expert, hidden_width, full_width)
    gate_part = jnp.einsum(
        "gocd,opfd->gopcf",
        arrived,
        w_gate.reshape(weight_shape),
        preferred_element_type=jnp.float32,
    )
    up_part = jnp.einsum(
        "gocd,opfd->gopcf", arrived, w_up.reshape(weight_shape), preferred_element_type=jnp.float32
    )
    hidden = (jax.nn.silu(gate_part) * up_part).astype(jnp.bfloat16)
    expert_parts = jnp.einsum(
        "gopcf,opfd->gopcd",
        hidden,
        w_down.reshape(weight_shape),
        preferred_element_type=jnp.float32,
    ).astype(jnp.bfloat16)
    returned = lax.all_to_all(expert_parts, "dp", split_axis=0, concat_axis=0, tiled=True)
    merged = jnp.sum(returned.astype(jnp.float32), axis=2).reshape(
        groups * own_experts * CAP, full_width
    )
    home_group = flat_ids // group_experts
    local_index = flat_ids % group_experts - first_expert
    present = (local_index >= 0) & (local_index < own_experts)
    clipped = jnp.clip(local_index, 0, own_experts - 1)
    lookup = (home_group * own_experts + clipped) * CAP + position
    factor = jnp.where(present, route_weights.reshape(-1), 0.0)
    picked = merged[lookup] * factor[:, None]
    mixed_rows = jnp.sum(picked.reshape(row_count, top_count, full_width), axis=1)
    summed = lax.psum_scatter(mixed_rows, "loop", scatter_dimension=1, tiled=True)
    return (values + summed).astype(jnp.bfloat16)


def solution(mesh):
    return jax.shard_map(
        shards,
        mesh=mesh,
        in_specs=(
            P("dp", "loop"),
            P(),
            P("dp", None),
            P("dp", None),
            P(("dp", "loop"), None, None),
            P(("dp", "loop"), None, None),
            P(("dp", "loop"), None, None),
        ),
        out_specs=P("dp", "loop"),
        check_vma=False,
    )
```

profile of v0, /device:TPU:25, one launch (start us, length us, event | category | flops | bytes accessed | tf_op | source)
XLA Modules:
  0.0 284.1 jit_solution(6171662056558365765)
XLA Ops:
  6.5 0.8 copy.18
  7.4 0.1 eq.31
  7.5 0.1 eq.27
  7.5 0.1 reshape.267
  7.7 0.1 copy.21
  7.8 0.2 fusion.11
  8.1 0.1 copy.22
  8.2 0.4 fusion.10
  8.6 4.3 %scatter_custom_fusion = s32[2048]{0:T(1024)S(1)} fusion(s32[1024]{0:T(1024)S(1)} %bitcast.75, s32[1024]{0:T(1024)S(1)} %add_select_fusion.1, s32[]{:T(128)} %constant.81.clone.1), kind=kCustom, calls=%fused_computation.61 | custom fusion | bytes 8196 | tf_op jit(solution)/shard_map/scatter | solution.py:32
  12.9 0.1 reshape.269
  13.1 0.1 reshape.276
  13.2 0.6 gather_fusion
  13.8 0.1 reshape.284
  13.9 0.1 fusion.13
  14.0 6.4 %psum.7 = f32[128]{0:T(128)S(1)} all-reduce(f32[128]{0:T(128)S(1)} %fusion.13), channel_id=1, replica_groups=mesh['dp'=8,'loop'=4] {'loop'}, use_global_device_ids=true, to_apply=%region_1.2 | all-reduce | flops 128 | bytes 1024 | tf_op jit(solution)/shard_map/psum | solution.py:22
  20.4 0.8 dynamic-slice_convert_fusion
  21.2 0.1 fusion.15
  21.3 12.6 %all_gather.3 = bf16[128,2048]{1,0:T(8,128)(2,1)S(1)} all-gather(bf16[128,512]{1,0:T(8,128)(2,1)S(1)} %fusion.15), channel_id=1, replica_groups=mesh['dp'=8,'loop'=4] {'loop'}, dimensions={1}, use_global_device_ids=true | all-gather | bytes 655360 | tf_op jit(solution)/shard_map/all_gather | solution.py:36
  33.9 2.5 gather_fusion.1
  36.4 34.4 %all_to_all.10 = bf16[8,4,16,2048]{3,2,1,0:T(8,128)(2,1)} all-to-all(bf16[8,4,16,2048]{3,2,1,0:T(8,128)(2,1)S(1)} %bitcast.71), channel_id=1, replica_groups=mesh['dp'=8,'loop'=4] {'dp'}, dimensions={0} | all-to-all | bytes 4194304 | tf_op jit(solution)/shard_map/all_to_all | solution.py:44
  70.7 15.0 %fusion.5 = f32[4,8,16,4,384]{4,2,3,1,0:T(8,128)} fusion(bf16[4,4,384,2048,1]{3,2,1,4,0:T(8,128)(2,1)} %bitcast.76, bf16[8,4,16,2048]{3,2,1,0:T(8,128)(2,1)} %all_to_all.10), kind=kOutput, calls=%fused_computation.15 | convolution fusion | flops 3221225472 | bytes 30408704 | tf_op jit(solution)/shard_map/gocd,opfd->gopcf/dot_general | solution.py:52
  85.8 14.6 %fusion.1 = bf16[8,4,4,16,384]{4,3,2,0,1:T(8,128)(2,1)} fusion(f32[4,8,16,4,384]{4,2,3,1,0:T(8,128)} %fusion.5, bf16[4,4,384,2048,1]{3,2,1,4,0:T(8,128)(2,1)} %bitcast.77, bf16[8,4,16,2048]{3,2,1,0:T(8,128)(2,1)S(1)} %copy-done), kind=kOutput, calls=%fused_computation.9 | convolution fusion | flops 3225944064 | bytes 31981568 | tf_op jit(solution)/shard_map/gocd,opfd->gopcf/dot_general | solution.py:46
  100.4 16.4 %convert_bitcast_fusion = bf16[8,4,4,16,2048]{4,3,0,2,1:T(8,128)(2,1)} fusion(bf16[4,4,384,2048,1]{3,2,4,1,0:T(8,128)(2,1)} %bitcast.70, bf16[8,4,4,16,384]{4,3,2,0,1:T(8,128)(2,1)} %fusion.1), kind=kOutput, calls=%fused_computation.7 | convolution fusion | flops 3225419776 | bytes 35127296 | tf_op jit(solution)/shard_map/gopcf,opfd->gopcd/dot_general | solution.py:56
  116.8 8.3 %copy.26 = bf16[8,4,4,16,2048]{4,3,2,1,0:T(8,128)(2,1)} copy(bf16[8,4,4,16,2048]{4,3,0,2,1:T(8,128)(2,1)} %convert_bitcast_fusion) | data formatting | bytes 16777216 | tf_op jit(solution)/shard_map/convert_element_type | solution.py:61
  125.0 6.3 %all-to-all-start.1 = ((bf16[8,4,4,16,2048]{4,3,2,1,0:T(8,128)(2,1)}), bf16[8,4,4,16,2048]{4,3,2,1,0:T(8,128)(2,1)}, u32[]{:S(2)}, u32[]{:S(2)}) async-start(bf16[8,4,4,16,2048]{4,3,2,1,0:T(8,128)(2,1)} %copy.26), calls=%async_computation.1 | async-start | bytes 16777216 | tf_op jit(solution)/shard_map/all_to_all | solution.py:62
  131.4 0.1 copy.29
  131.5 90.4 %all-to-all-done.1 = bf16[8,4,4,16,2048]{4,3,2,1,0:T(8,128)(2,1)} async-done(((bf16[8,4,4,16,2048]{4,3,2,1,0:T(8,128)(2,1)}), bf16[8,4,4,16,2048]{4,3,2,1,0:T(8,128)(2,1)}, u32[]{:S(2)}, u32[]{:S(2)}) %all-to-all-start.1) | async-done | bytes 8388640 | tf_op jit(solution)/shard_map/all_to_all | solution.py:62
  221.9 7.7 %convert_reduce_fusion = f32[8,4,16,2048]{3,2,1,0:T(8,128)} fusion(bf16[8,4,4,16,2048]{4,3,2,1,0:T(8,128)(2,1)} %all-to-all-done.1), kind=kLoop, calls=%fused_computation.4 | loop fusion | flops 7340032 | bytes 12582912 | tf_op jit(solution)/shard_map/reduce_sum | solution.py:63
  229.6 11.2 %gather_fusion.2 = f32[1024,2048]{1,0:T(8,128)} fusion(f32[512,2048]{1,0:T(8,128)} %bitcast.69, s32[1024]{0:T(1024)S(1)} %broadcast_clamp_fusion), kind=kCustom, calls=%fused_computation.2 | custom fusion | bytes 16781312 | tf_op jit(solution)/shard_map/gather | solution.py:72
  240.7 7.5 %fusion = f32[128,2048]{1,0:T(8,128)} fusion(f32[1024,2048]{1,0:T(8,128)} %gather_fusion.2, f32[128,8]{1,0:T(8,128)S(1)} %copy.29), kind=kLoop, calls=%fused_computation.6 | loop fusion | flops 3932160 | bytes 9441280 | tf_op jit(solution)/shard_map/reduce_sum | solution.py:73
  248.3 27.3 %reduce-scatter.2.cloned.1.call-done = f32[128,512]{1,0:T(8,128)} async-done(((f32[128,2048]{1,0:T(8,128)}), f32[128,512]{1,0:T(8,128)}) %reduce-scatter.2.cloned.1.call-update) | async-done | bytes 262160 | tf_op jit(solution)/shard_map/reduce_scatter | solution.py:74
  275.6 1.6 fusion.16
  (25 shorter events, 0.3 us)
Async XLA Ops:
  6.5 7.3 %copy-start.1 = (bf16[128,512]{1,0:T(8,128)(2,1)S(1)}, bf16[128,512]{1,0:T(8,128)(2,1)}, u32[]{:S(2)}) copy-start(bf16[128,512]{1,0:T(8,128)(2,1)} %param.7) | copy-start | bytes 393220
  70.7 15.0 %copy-start = (bf16[8,4,16,2048]{3,2,1,0:T(8,128)(2,1)S(1)}, bf16[8,4,16,2048]{3,2,1,0:T(8,128)(2,1)}, u32[]{:S(2)}) copy-start(bf16[8,4,16,2048]{3,2,1,0:T(8,128)(2,1)} %all_to_all.10) | copy-start | bytes 6291460
  125.0 6.3 %copy-start.2 = (s32[128,8]{0,1:T(8,128)S(1)}, s32[128,8]{0,1:T(8,128)}, u32[]{:S(2)}) copy-start(s32[128,8]{0,1:T(8,128)} %param.9) | copy-start | bytes 12292
  125.0 6.3 %copy-start.3 = (f32[128,8]{0,1:T(8,128)S(1)}, f32[128,8]{0,1:T(8,128)}, u32[]{:S(2)}) copy-start(f32[128,8]{0,1:T(8,128)} %param.10) | copy-start | bytes 12292
  125.0 96.9 %all-to-all-start.1 = ((bf16[8,4,4,16,2048]{4,3,2,1,0:T(8,128)(2,1)}), bf16[8,4,4,16,2048]{4,3,2,1,0:T(8,128)(2,1)}, u32[]{:S(2)}, u32[]{:S(2)}) async-start(bf16[8,4,4,16,2048]{4,3,2,1,0:T(8,128)(2,1)} %copy.26), calls=%async_computation.1 | async-start | bytes 16777216 | tf_op jit(solution)/shard_map/all_to_all | solution.py:62
  131.3 144.3 %reduce-scatter.2.cloned.1.call-start = ((), (), s32[]{:S(2)}) async-start(), calls=%async_computation.3 | async-start | bytes 1310720 | tf_op jit(solution)/shard_map/reduce_scatter | solution.py:74
Sparse Core Ops, SparseCore 0:
  248.4 27.1 reduce-scatter.1
where the time goes:
time: 289 us; the launch traced here: 284 us
  waiting for transfers between devices  118 us (41%)
  blocking collectives  53.4 us (18%)
  matrix products  46 us (16%)
  local copies, waits for them, and re-layouts  28.5 us (10%)
  other arithmetic  18.6 us (6%)
  between operations  13.6 us (5%)
  starting transfers between devices  6.3 us (2%)
    all_to_all x1, waiting for transfers between devices, shards(): lax.all_to_all(expert_parts, 'dp', split_axis=0, concat_axis=0, tiled=True)  90.4 us
    all_to_all x1, blocking collectives, shards(): lax.all_to_all(send_rows, 'dp', split_axis=0, concat_axis=0, tiled=True)  34.4 us
    reduce_scatter x1, waiting for transfers between devices, shards(): lax.psum_scatter(mixed_rows, 'loop', scatter_dimension=1, tiled=True)  27.3 us
    dot_general x1, matrix products, shards(): jnp.einsum('gopcf,opfd->gopcd', hidden, w_down.reshape(weight_shape), pre...  16.4 us
    dot_general x1, matrix products, shards(): jnp.einsum('gocd,opfd->gopcf', arrived, w_up.reshape(weight_shape), prefe...  15 us
    dot_general x1, matrix products, shards(): jnp.einsum('gocd,opfd->gopcf', arrived, w_gate.reshape(weight_shape), pre...  14.6 us
    all_gather x1, blocking collectives, shards(): full_rows = lax.all_gather(normed, 'loop', axis=1, tiled=True)  12.6 us
    gather x1, local copies, waits for them, and re-layouts, shards(): picked = merged[lookup] * factor[:, None]  11.2 us
  transfers between devices with their start and end apart: 2, of which 2 were waited for; matrix products, arithmetic and copies ran while one was open for 0% of the time, Pallas kernels for 0%

commit v1 on v0

v1 whole, which is shorter than its diff:
```python
import functools

import jax
import jax.numpy as jnp
from jax import lax
from jax.experimental import pallas as pl
from jax.experimental.pallas import tpu as pltpu
from jax.sharding import PartitionSpec as P

HGROUPS = 4
CAP = 16
SLOTS = 8
COLUMNS = 512
MESH = pl.DeviceIdType.MESH


def kernel(
    sizes,
    tokens_ref,
    gain_ref,
    ids_ref,
    factor_ref,
    gate_hbm,
    up_hbm,
    down_hbm,
    out_ref,
    full,
    normed,
    place,
    mix_high,
    mix_low,
    outgoing,
    arrived,
    hidden,
    results,
    returned,
    partial,
    landed,
    gate_buf,
    up_buf,
    down_buf,
    gate_sem,
    up_sem,
    down_sem,
    row_send,
    row_recv,
    go_send,
    go_recv,
    back_send,
    back_recv,
    part_send,
    part_recv,
):
    groups, loops, own, per, slots = sizes
    pairs = own * per
    rows, width = tokens_ref.shape
    full_width = loops * width
    block = groups * CAP
    top = ids_ref.shape[1]
    mine = lax.axis_index("dp")
    spot = lax.axis_index("loop")

    def gate_copy(pair):
        slot = lax.rem(pair, slots)
        return pltpu.make_async_copy(gate_hbm.at[pair], gate_buf.at[slot], gate_sem.at[slot])

    def up_copy(pair):
        slot = lax.rem(pair, slots)
        return pltpu.make_async_copy(up_hbm.at[pair], up_buf.at[slot], up_sem.at[slot])

    def down_copy(pair):
        slot = lax.rem(pair, slots)
        return pltpu.make_async_copy(down_hbm.at[pair], down_buf.at[slot], down_sem.at[slot])

    def row_copy(owner, target):
        return pltpu.make_async_remote_copy(
            src_ref=tokens_ref,
            dst_ref=full.at[owner],
            send_sem=row_send.at[target],
            recv_sem=row_recv.at[owner],
            device_id=(mine, target),
            device_id_type=MESH,
        )

    def go_copy(expert, owner, target):
        return pltpu.make_async_remote_copy(
            src_ref=outgoing.at[expert, target],
            dst_ref=arrived.at[expert, owner],
            send_sem=go_send.at[expert, target],
            recv_sem=go_recv.at[expert, owner],
            device_id=(target, spot),
            device_id_type=MESH,
        )

    def back_copy(expert, owner, target):
        return pltpu.make_async_remote_copy(
            src_ref=results.at[expert, target],
            dst_ref=returned.at[expert, owner],
            send_sem=back_send.at[expert, target],
            recv_sem=back_recv.at[expert, owner],
            device_id=(target, spot),
            device_id_type=MESH,
        )

    def part_copy(owner, target):
        return pltpu.make_async_remote_copy(
            src_ref=partial.at[target],
            dst_ref=landed.at[owner],
            send_sem=part_send.at[target],
            recv_sem=part_recv.at[owner],
            device_id=(mine, target),
            device_id_type=MESH,
        )

    def loop_peers(body):
        def step(i, carry):
            body(lax.rem(spot + i, loops))
            return carry

        lax.fori_loop(1, loops, step, 0)

    def dp_peers(body):
        def step(i, carry):
            body(lax.rem(mine + i, groups))
            return carry

        lax.fori_loop(1, groups, step, 0)

    barrier = pltpu.get_barrier_semaphore()
    loop_peers(
        lambda peer: pl.semaphore_signal(
            barrier, inc=1, device_id=(mine, peer), device_id_type=MESH
        )
    )
    dp_peers(
        lambda peer: pl.semaphore_signal(
            barrier, inc=1, device_id=(peer, spot), device_id_type=MESH
        )
    )
    pl.semaphore_wait(barrier, loops + groups - 2)
    loop_peers(lambda peer: row_copy(spot, peer).start())

    def prefetch(pair, carry):
        gate_copy(pair).start()
        up_copy(pair).start()
        down_copy(pair).start()
        return carry

    lax.fori_loop(0, slots, prefetch, 0)

    total_slots = own * block
    column = lax.broadcasted_iota(jnp.int32, (rows, total_slots), 1)
    owner = lax.rem(column, block) // CAP
    first = spot * pairs // HGROUPS
    expert_of = owner * (pairs * loops // HGROUPS) + first + column // block
    chosen = jnp.zeros((rows, total_slots), jnp.float32)
    factor = jnp.zeros((rows, total_slots), jnp.float32)
    for k in range(top):
        hit = ids_ref[:, k : k + 1] == expert_of
        chosen = jnp.where(hit, 1.0, chosen)
        factor = jnp.where(hit, factor_ref[:, k : k + 1], factor)
    earlier = (
        lax.broadcasted_iota(jnp.int32, (rows, rows), 1)
        < lax.broadcasted_iota(jnp.int32, (rows, rows), 0)
    ).astype(jnp.float32)
    rank = jnp.dot(
        earlier.astype(jnp.bfloat16),
        chosen.astype(jnp.bfloat16),
        preferred_element_type=jnp.float32,
    )
    here = jnp.where(rank == lax.rem(column, CAP).astype(jnp.float32), chosen, 0.0)
    factor = factor * here
    high = factor.astype(jnp.bfloat16)
    place[...] = here.astype(jnp.bfloat16)
    mix_high[...] = high
    mix_low[...] = (factor - high.astype(jnp.float32)).astype(jnp.bfloat16)

    full[spot] = tokens_ref[...]
    loop_peers(lambda peer: row_copy(peer, peer).wait_recv())
    square = jnp.zeros((rows, 1), jnp.float32)
    for j in range(loops):
        values = full[j].astype(jnp.float32)
        square = square + jnp.sum(values * values, axis=1, keepdims=True)
    row_scale = lax.rsqrt(square / full_width + 1e-06)
    for j in range(loops):
        columns = pl.ds(j * width, width)
        gain = gain_ref[:, columns].astype(jnp.float32)
        normed[:, columns] = (full[j].astype(jnp.float32) * row_scale * gain).astype(jnp.bfloat16)

    for o in range(own):
        picked = lax.dot_general(
            place[:, o * block : (o + 1) * block],
            normed[...],
            (((0,), (0,)), ((), ())),
            preferred_element_type=jnp.float32,
        ).astype(jnp.bfloat16)
        outgoing[o] = picked.reshape(groups, CAP, full_width)
        dp_peers(lambda peer: go_copy(o, mine, peer).start())
        arrived[o, mine] = outgoing[o, mine]

    def expert_step(o, carry):
        dp_peers(lambda peer: go_copy(o, peer, peer).wait_recv())

        def pair_step(h, inner):
            pair = o * per + h
            slot = lax.rem(pair, slots)
            batch = arrived[o].reshape(block, full_width)
            gate_copy(pair).wait()
            up_copy(pair).wait()
            contract = (((1,), (1,)), ((), ()))
            gate = lax.dot_general(
                batch, gate_buf[slot], contract, preferred_element_type=jnp.float32
            )
            up = lax.dot_general(batch, up_buf[slot], contract, preferred_element_type=jnp.float32)
            hidden[h] = (gate / (1.0 + jnp.exp(-gate)) * up).astype(jnp.bfloat16)

            @pl.when(pair + slots < pairs)
            def _():
                gate_copy(pair + slots).start()
                up_copy(pair + slots).start()

            return inner

        lax.fori_loop(0, per, pair_step, 0)
        for h in range(per):
            down_copy(o * per + h).wait()
        for c in range(full_width // COLUMNS):
            columns = pl.ds(c * COLUMNS, COLUMNS)
            total = None
            for h in range(per):
                slot = lax.rem(o * per + h, slots)
                term = jnp.dot(
                    hidden[h], down_buf[slot, :, columns], preferred_element_type=jnp.float32
                )
                total = term if total is None else total + term
            results[o, :, :, columns] = total.astype(jnp.bfloat16).reshape(groups, CAP, COLUMNS)
        for h in range(per):

            @pl.when(o * per + h + slots < pairs)
            def _():
                down_copy(o * per + h + slots).start()

        dp_peers(lambda peer: back_copy(o, mine, peer).start())
        returned[o, mine] = results[o, mine]
        return carry

    lax.fori_loop(0, own, expert_step, 0)

    def expert_wait(o, carry):
        dp_peers(lambda peer: back_copy(o, peer, peer).wait_recv())
        return carry

    lax.fori_loop(0, own, expert_wait, 0)
    for j in range(loops):
        columns = pl.ds(j * width, width)
        rows_back = returned[:, :, :, columns].reshape(total_slots, width)
        mixed = jnp.dot(mix_high[...], rows_back, preferred_element_type=jnp.float32)
        mixed = mixed + jnp.dot(mix_low[...], rows_back, preferred_element_type=jnp.float32)
        partial[j] = mixed.astype(jnp.bfloat16)

        @pl.when(spot != j)
        def _():
            part_copy(spot, j).start()

    landed[spot] = partial[spot]
    loop_peers(lambda peer: part_copy(peer, peer).wait_recv())
    total = tokens_ref[...].astype(jnp.float32)
    for j in range(loops):
        total = total + landed[j].astype(jnp.float32)
    out_ref[...] = total.astype(out_ref.dtype)

    loop_peers(lambda peer: row_copy(spot, peer).wait_send())
    loop_peers(lambda peer: part_copy(spot, peer).wait_send())

    def drain(o, carry):
        dp_peers(lambda peer: go_copy(o, mine, peer).wait_send())
        dp_peers(lambda peer: back_copy(o, mine, peer).wait_send())
        return carry

    lax.fori_loop(0, own, drain, 0)


def shards(tokens, norm_gain, route_ids, route_weights, w_gate, w_up, w_down):
    rows, width = tokens.shape
    groups, loops = lax.axis_size("dp"), lax.axis_size("loop")
    pairs, hidden_width, full_width = w_gate.shape
    own = max(1, pairs // HGROUPS)
    per = pairs // own
    slots = min(SLOTS, pairs)
    block = groups * CAP
    half, single = jnp.bfloat16, jnp.float32
    vmem = pl.BlockSpec(memory_space=pltpu.VMEM)
    anywhere = pl.BlockSpec(memory_space=pl.ANY)
    dma = pltpu.SemaphoreType.DMA
    weights = pltpu.VMEM((slots, hidden_width, full_width), half)
    exchange = pltpu.VMEM((own, groups, CAP, full_width), half)
    return pl.pallas_call(
        functools.partial(kernel, (groups, loops, own, per, slots)),
        out_shape=jax.ShapeDtypeStruct((rows, width), half),
        in_specs=[vmem] * 4 + [anywhere] * 3,
        out_specs=vmem,
        scratch_shapes=[
            pltpu.VMEM((loops, rows, width), half),
            pltpu.VMEM((rows, full_width), half),
            pltpu.VMEM((rows, own * block), half),
            pltpu.VMEM((rows, own * block), half),
            pltpu.VMEM((rows, own * block), half),
            exchange,
            exchange,
            pltpu.VMEM((per, block, hidden_width), half),
            exchange,
            exchange,
            pltpu.VMEM((loops, rows, width), half),
            pltpu.VMEM((loops, rows, width), half),
            weights,
            weights,
            weights,
            dma((slots,)),
            dma((slots,)),
            dma((slots,)),
            dma((loops,)),
            dma((loops,)),
            dma((own, groups)),
            dma((own, groups)),
            dma((own, groups)),
            dma((own, groups)),
            dma((loops,)),
            dma((loops,)),
        ],
        compiler_params=pltpu.CompilerParams(
            collective_id=0, has_side_effects=True, vmem_limit_bytes=60 * 1024 * 1024
        ),
        cost_estimate=pl.CostEstimate(
            flops=6 * pairs * block * hidden_width * full_width,
            bytes_accessed=6 * pairs * hidden_width * full_width,
            transcendentals=pairs * block * hidden_width,
        ),
    )(tokens, norm_gain.reshape(1, full_width), route_ids, route_weights, w_gate, w_up, w_down)


def solution(mesh):
    return jax.shard_map(
        shards,
        mesh=mesh,
        in_specs=(
            P("dp", "loop"),
            P(),
            P("dp", None),
            P("dp", None),
            P(("dp", "loop"), None, None),
            P(("dp", "loop"), None, None),
            P(("dp", "loop"), None, None),
        ),
        out_specs=P("dp", "loop"),
        check_vma=False,
    )
```

time: 289 us -> 85.8 us (0.30); the launches traced: 284 us -> 85.5 us
  waiting for transfers between devices: 118 us -> 0 us
  Pallas kernels: 0 us -> 79.8 us
  blocking collectives: 53.4 us -> 0 us
  matrix products: 46 us -> 0 us
  local copies, waits for them, and re-layouts: 28.5 us -> 5.67 us
  other arithmetic: 18.6 us -> 0 us
  between operations: 13.6 us -> 0.01 us
  starting transfers between devices: 6.3 us -> 0 us
    all_to_all x1 -> x0, waiting for transfers between devices: 90.4 us -> none  [shards(): lax.all_to_all(expert_parts, 'dp', split_axis=0, concat_axis=0, tiled=True)]
    pallas_call x0 -> x1, Pallas kernels: none -> 79.8 us  [shards(): pl.pallas_call(functools.partial(kernel, (groups, loops, own, per, slots)...]
    dot_general x3 -> x0, matrix products: 46 us -> none  [the longest x1 16.4 us: shards(): jnp.einsum('gopcf,opfd->gopcd', hidden, w_down.reshape(weight_shape), pre...]
    all_to_all x1 -> x0, blocking collectives: 34.4 us -> none  [shards(): lax.all_to_all(send_rows, 'dp', split_axis=0, concat_axis=0, tiled=True)]
    reduce_scatter x1 -> x0, waiting for transfers between devices: 27.3 us -> none  [shards(): lax.psum_scatter(mixed_rows, 'loop', scatter_dimension=1, tiled=True)]
    reduce_sum x4 -> x0, other arithmetic: 15.7 us -> none  [the longest x1 7.69 us: shards(): jnp.sum(returned.astype(jnp.float32), axis=2)]
    gather x3 -> x0, local copies, waits for them, and re-layouts: 14.2 us -> none  [the longest x1 11.2 us: shards(): picked = merged[lookup] * factor[:, None]]
    all_gather x1 -> x0, blocking collectives: 12.6 us -> none  [shards(): full_rows = lax.all_gather(normed, 'loop', axis=1, tiled=True)]
  transfers between devices with their start and end apart: 2 -> 0, of which waited for: 2 -> 0; matrix products, arithmetic and copies ran while one was open for 0% -> 0% of each run, Pallas kernels for 0% -> 0%
where the time goes in v1:
time: 85.8 us; the launch traced here: 85.5 us
  Pallas kernels  79.8 us (93%)
  local copies, waits for them, and re-layouts  5.67 us (7%)
    pallas_call x1, Pallas kernels, shards(): pl.pallas_call(functools.partial(kernel, (groups, loops, own, per, slots)...  79.8 us
    unnamed x3, local copies, waits for them, and re-layouts  4.39 us

profile of v1, /device:TPU:25, one launch (start us, length us, event | category | flops | bytes accessed | tf_op | source)
XLA Modules:
  0.0 85.5 jit_solution(9677014395849500013)
XLA Ops:
  0.0 1.3 %reshape.3.gain_ref = bf16[1,2048]{1,0:T(2,128)(2,1)} reshape(bf16[2048]{0:T(1024)(128)(2,1)} %param.8) | data formatting | bytes 8192 | tf_op jit(solution)/shard_map/reshape | solution.py:338
  1.3 1.4 %copy.8.ids_ref = s32[128,8]{1,0:T(8,128)} copy(s32[128,8]{0,1:T(8,128)} %param.9) | data formatting | bytes 8192 | tf_op args[2]
  2.7 1.4 %copy.9.factor_ref = f32[128,8]{1,0:T(8,128)} copy(f32[128,8]{0,1:T(8,128)} %param.10) | data formatting | bytes 8192 | tf_op args[3]
  4.1 79.8 %shard_map.73 = bf16[128,512]{1,0:T(8,128)(2,1)} custom-call(bf16[128,512]{1,0:T(8,128)(2,1)} %tokens_ref.1, bf16[1,2048]{1,0:T(2,128)(2,1)} %reshape.3.gain_ref, s32[128,8]{1,0:T(8,128)} %copy.8.ids_ref, f32[128,8]{1,0:T(8,128)} %copy.9.factor_ref, bf16[16,384,2048]{2,1,0:T(8,128)(2,1)} %gate_hbm.1, bf16[16,384,2048]{2,1,0:T(8,128)(2,1)} %up_hbm.1, ...), custom_call_target="tpu_custom_call" | custom-call | flops 9663676416 | bytes 75497472 | tf_op jit(solution)/shard_map/pallas_call | solution.py:297
  83.9 1.6 %copy.11 = bf16[128,512]{1,0:T(8,128)(2,1)} copy(bf16[128,512]{1,0:T(8,128)(2,1)} %shard_map.73) | data formatting | bytes 262144

commit v2 on v1

--- a/solution.py
+++ b/solution.py
@@ -10,7 +10,7 @@
 HGROUPS = 4
 CAP = 16
 SLOTS = 8
-COLUMNS = 512
+PIECES = 4
 MESH = pl.DeviceIdType.MESH
 
 
@@ -25,12 +25,14 @@
     down_hbm,
     out_ref,
     full,
-    normed,
+    batch,
     place,
     mix_high,
     mix_low,
-    outgoing,
-    arrived,
+    near_out,
+    near,
+    far_out,
+    far,
     hidden,
     results,
     returned,
@@ -44,10 +46,14 @@
     down_sem,
     row_send,
     row_recv,
-    go_send,
-    go_recv,
+    near_send,
+    near_recv,
+    far_send,
+    far_recv,
     back_send,
     back_recv,
+    piece_send,
+    piece_recv,
     part_send,
     part_recv,
 ):
@@ -57,6 +63,8 @@
     full_width = loops * width
     block = groups * CAP
     top = ids_ref.shape[1]
+    pieces = min(PIECES, loops)
+    share = loops // pieces
     mine = lax.axis_index("dp")
     spot = lax.axis_index("loop")
 
@@ -82,12 +90,22 @@
             device_id_type=MESH,
         )
 
-    def go_copy(expert, owner, target):
-        return pltpu.make_async_remote_copy(
-            src_ref=outgoing.at[expert, target],
-            dst_ref=arrived.at[expert, owner],
-            send_sem=go_send.at[expert, target],
-            recv_sem=go_recv.at[expert, owner],
+    def near_copy(owner, target):
+        return pltpu.make_async_remote_copy(
+            src_ref=near_out.at[target],
+            dst_ref=near.at[owner],
+            send_sem=near_send.at[target],
+            recv_sem=near_recv.at[owner],
+            device_id=(target, spot),
+            device_id_type=MESH,
+        )
+
+    def far_copy(expert, owner, target):
+        return pltpu.make_async_remote_copy(
+            src_ref=far_out.at[expert, target],
+            dst_ref=far.at[expert, owner],
+            send_sem=far_send.at[expert, target],
+            recv_sem=far_recv.at[expert, owner],
             device_id=(target, spot),
             device_id_type=MESH,
         )
@@ -102,6 +120,20 @@
             device_id_type=MESH,
         )
 
+    def piece_columns(c):
+        piece = lax.rem(spot // share + 1 + c, pieces)
+        return pl.ds(pl.multiple_of(piece * share * width, share * width), share * width)
+
+    def piece_copy(c, owner, target):
+        return pltpu.make_async_remote_copy(
+            src_ref=results.at[own - 1, target, :, piece_columns(c)],
+            dst_ref=returned.at[own - 1, owner, :, piece_columns(c)],
+            send_sem=piece_send.at[c, target],
+            recv_sem=piece_recv.at[c, owner],
+            device_id=(target, spot),
+            device_id_type=MESH,
+        )
+
     def part_copy(owner, target):
         return pltpu.make_async_remote_copy(
             src_ref=partial.at[target],
@@ -137,8 +169,6 @@
             barrier, inc=1, device_id=(peer, spot), device_id_type=MESH
         )
     )
-    pl.semaphore_wait(barrier, loops + groups - 2)
-    loop_peers(lambda peer: row_copy(spot, peer).start())
 
     def prefetch(pair, carry):
         gate_copy(pair).start()
@@ -175,43 +205,59 @@
     mix_high[...] = high
     mix_low[...] = (factor - high.astype(jnp.float32)).astype(jnp.bfloat16)
 
-    full[spot] = tokens_ref[...]
+    gathering = (((0,), (0,)), ((), ()))
+    picked = lax.dot_general(
+        place[...], tokens_ref[...], gathering, preferred_element_type=jnp.float32
+    ).astype(jnp.bfloat16)
+    picked = picked.reshape(own, groups, CAP, width)
+    for o in range(own):
+        near_out[:, o] = picked[o]
+    pl.semaphore_wait(barrier, loops + groups - 2)
+    loop_peers(lambda peer: row_copy(spot, peer).start())
+    dp_peers(lambda peer: near_copy(mine, peer).start())
+    near[mine] = near_out[mine]
+
     loop_peers(lambda peer: row_copy(peer, peer).wait_recv())
-    square = jnp.zeros((rows, 1), jnp.float32)
-    for j in range(loops):
-        values = full[j].astype(jnp.float32)
-        square = square + jnp.sum(values * values, axis=1, keepdims=True)
-    row_scale = lax.rsqrt(square / full_width + 1e-06)
-    for j in range(loops):
-        columns = pl.ds(j * width, width)
-        gain = gain_ref[:, columns].astype(jnp.float32)
-        normed[:, columns] = (full[j].astype(jnp.float32) * row_scale * gain).astype(jnp.bfloat16)
-
     for o in range(own):
-        picked = lax.dot_general(
-            place[:, o * block : (o + 1) * block],
-            normed[...],
-            (((0,), (0,)), ((), ())),
-            preferred_element_type=jnp.float32,
-        ).astype(jnp.bfloat16)
-        outgoing[o] = picked.reshape(groups, CAP, full_width)
-        dp_peers(lambda peer: go_copy(o, mine, peer).start())
-        arrived[o, mine] = outgoing[o, mine]
+        for i in range(1, loops):
+            picked = lax.dot_general(
+                place[:, o * block : (o + 1) * block],
+                full[lax.rem(spot + i, loops)],
+                gathering,
+                preferred_element_type=jnp.float32,
+            ).astype(jnp.bfloat16)
+            far_out[o, :, i - 1] = picked.reshape(groups, CAP, width)
+        dp_peers(lambda peer: far_copy(o, mine, peer).start())
+        far[o, mine] = far_out[o, mine]
+
+    dp_peers(lambda peer: near_copy(peer, peer).wait_recv())
 
     def expert_step(o, carry):
-        dp_peers(lambda peer: go_copy(o, peer, peer).wait_recv())
+        dp_peers(lambda peer: far_copy(o, peer, peer).wait_recv())
+        square = jnp.zeros((block, 1), jnp.float32)
+        for i in range(loops):
+            raw = near[:, o] if i == 0 else far[o, :, i - 1]
+            values = raw.reshape(block, width).astype(jnp.float32)
+            square = square + jnp.sum(values * values, axis=1, keepdims=True)
+        row_scale = lax.rsqrt(square / full_width + 1e-06)
+        for i in range(loops):
+            raw = near[:, o] if i == 0 else far[o, :, i - 1]
+            values = raw.reshape(block, width).astype(jnp.float32)
+            columns = pl.ds(pl.multiple_of(lax.rem(spot + i, loops) * width, width), width)
+            gain = gain_ref[:, columns].astype(jnp.float32)
+            batch[:, columns] = (values * row_scale * gain).astype(jnp.bfloat16)
 
         def pair_step(h, inner):
             pair = o * per + h
             slot = lax.rem(pair, slots)
-            batch = arrived[o].reshape(block, full_width)
+            normed = batch[...]
             gate_copy(pair).wait()
             up_copy(pair).wait()
             contract = (((1,), (1,)), ((), ()))
             gate = lax.dot_general(
-                batch, gate_buf[slot], contract, preferred_element_type=jnp.float32
+                normed, gate_buf[slot], contract, preferred_element_type=jnp.float32
             )
-            up = lax.dot_general(batch, up_buf[slot], contract, preferred_element_type=jnp.float32)
+            up = lax.dot_general(normed, up_buf[slot], contract, preferred_element_type=jnp.float32)
             hidden[h] = (gate / (1.0 + jnp.exp(-gate)) * up).astype(jnp.bfloat16)
 
             @pl.when(pair + slots < pairs)
@@ -224,8 +270,8 @@
         lax.fori_loop(0, per, pair_step, 0)
         for h in range(per):
             down_copy(o * per + h).wait()
-        for c in range(full_width // COLUMNS):
-            columns = pl.ds(c * COLUMNS, COLUMNS)
+        for c in range(pieces):
+            columns = piece_columns(c)
             total = None
             for h in range(per):
                 slot = lax.rem(o * per + h, slots)
@@ -233,14 +279,24 @@
                     hidden[h], down_buf[slot, :, columns], preferred_element_type=jnp.float32
                 )
                 total = term if total is None else total + term
-            results[o, :, :, columns] = total.astype(jnp.bfloat16).reshape(groups, CAP, COLUMNS)
+            results[o, :, :, columns] = total.astype(jnp.bfloat16).reshape(
+                groups, CAP, share * width
+            )
+
+            @pl.when(o == own - 1)
+            def _():
+                dp_peers(lambda peer: piece_copy(c, mine, peer).start())
+
         for h in range(per):
 
             @pl.when(o * per + h + slots < pairs)
             def _():
                 down_copy(o * per + h + slots).start()
 
-        dp_peers(lambda peer: back_copy(o, mine, peer).start())
+        @pl.when(o < own - 1)
+        def _():
+            dp_peers(lambda peer: back_copy(o, mine, peer).start())
+
         returned[o, mine] = results[o, mine]
         return carry
 
@@ -250,17 +306,20 @@
         dp_peers(lambda peer: back_copy(o, peer, peer).wait_recv())
         return carry
 
-    lax.fori_loop(0, own, expert_wait, 0)
-    for j in range(loops):
-        columns = pl.ds(j * width, width)
-        rows_back = returned[:, :, :, columns].reshape(total_slots, width)
-        mixed = jnp.dot(mix_high[...], rows_back, preferred_element_type=jnp.float32)
-        mixed = mixed + jnp.dot(mix_low[...], rows_back, preferred_element_type=jnp.float32)
-        partial[j] = mixed.astype(jnp.bfloat16)
-
-        @pl.when(spot != j)
-        def _():
-            part_copy(spot, j).start()
+    lax.fori_loop(0, own - 1, expert_wait, 0)
+    for c in range(pieces):
+        dp_peers(lambda peer: piece_copy(c, peer, peer).wait_recv())
+        for i in range(share):
+            target = lax.rem(spot // share + 1 + c, pieces) * share + i
+            columns = pl.ds(pl.multiple_of(target * width, width), width)
+            rows_back = returned[:, :, :, columns].reshape(total_slots, width)
+            mixed = jnp.dot(mix_high[...], rows_back, preferred_element_type=jnp.float32)
+            mixed = mixed + jnp.dot(mix_low[...], rows_back, preferred_element_type=jnp.float32)
+            partial[target] = mixed.astype(jnp.bfloat16)
+
+            @pl.when(target != spot)
+            def _():
+                part_copy(spot, target).start()
 
     landed[spot] = partial[spot]
     loop_peers(lambda peer: part_copy(peer, peer).wait_recv())
@@ -272,12 +331,20 @@
     loop_peers(lambda peer: row_copy(spot, peer).wait_send())
     loop_peers(lambda peer: part_copy(spot, peer).wait_send())
 
-    def drain(o, carry):
-        dp_peers(lambda peer: go_copy(o, mine, peer).wait_send())
+    dp_peers(lambda peer: near_copy(mine, peer).wait_send())
+
+    def drain_far(o, carry):
+        dp_peers(lambda peer: far_copy(o, mine, peer).wait_send())
+        return carry
+
+    def drain_back(o, carry):
         dp_peers(lambda peer: back_copy(o, mine, peer).wait_send())
         return carry
 
-    lax.fori_loop(0, own, drain, 0)
+    lax.fori_loop(0, own, drain_far, 0)
+    lax.fori_loop(0, own - 1, drain_back, 0)
+    for c in range(pieces):
+        dp_peers(lambda peer: piece_copy(c, mine, peer).wait_send())
 
 
 def shards(tokens, norm_gain, route_ids, route_weights, w_gate, w_up, w_down):
@@ -287,12 +354,15 @@
     own = max(1, pairs // HGROUPS)
     per = pairs // own
     slots = min(SLOTS, pairs)
+    pieces = min(PIECES, loops)
     block = groups * CAP
     half, single = jnp.bfloat16, jnp.float32
     vmem = pl.BlockSpec(memory_space=pltpu.VMEM)
     anywhere = pl.BlockSpec(memory_space=pl.ANY)
     dma = pltpu.SemaphoreType.DMA
     weights = pltpu.VMEM((slots, hidden_width, full_width), half)
+    near = pltpu.VMEM((groups, own, CAP, width), half)
+    far = pltpu.VMEM((own, groups, loops - 1, CAP, width), half)
     exchange = pltpu.VMEM((own, groups, CAP, full_width), half)
     return pl.pallas_call(
         functools.partial(kernel, (groups, loops, own, per, slots)),
@@ -301,12 +371,14 @@
         out_specs=vmem,
         scratch_shapes=[
             pltpu.VMEM((loops, rows, width), half),
-            pltpu.VMEM((rows, full_width), half),
+            pltpu.VMEM((block, full_width), half),
             pltpu.VMEM((rows, own * block), half),
             pltpu.VMEM((rows, own * block), half),
             pltpu.VMEM((rows, own * block), half),
-            exchange,
-            exchange,
+            near,
+            near,
+            far,
+            far,
             pltpu.VMEM((per, block, hidden_width), half),
             exchange,
             exchange,
@@ -320,10 +392,14 @@
             dma((slots,)),
             dma((loops,)),
             dma((loops,)),
+            dma((groups,)),
+            dma((groups,)),
             dma((own, groups)),
             dma((own, groups)),
             dma((own, groups)),
             dma((own, groups)),
+            dma((pieces, groups)),
+            dma((pieces, groups)),
             dma((loops,)),
             dma((loops,)),
         ],

time: 85.8 us -> 77.4 us (0.902)
  Pallas kernels: 79.8 us -> 71 us
    pallas_call x1, Pallas kernels: 79.8 us -> 71 us  [shards(): pl.pallas_call(functools.partial(kernel, (groups, loops, own, per, slots)...]
where the time goes in v2:
time: 77.4 us; the launch traced here: 76.7 us
  Pallas kernels  71 us (92%)
  local copies, waits for them, and re-layouts  5.67 us (7%)
    pallas_call x1, Pallas kernels, shards(): pl.pallas_call(functools.partial(kernel, (groups, loops, own, per, slots)...  71 us
    unnamed x3, local copies, waits for them, and re-layouts  4.39 us

profile of v2, /device:TPU:25, one launch (start us, length us, event | category | flops | bytes accessed | tf_op | source)
XLA Modules:
  0.0 76.7 jit_solution(14434787566468857273)
XLA Ops:
  0.0 1.3 %reshape.3.gain_ref = bf16[1,2048]{1,0:T(2,128)(2,1)} reshape(bf16[2048]{0:T(1024)(128)(2,1)} %param.8) | data formatting | bytes 8192 | tf_op jit(solution)/shard_map/reshape | solution.py:414
  1.3 1.4 %copy.8.ids_ref = s32[128,8]{1,0:T(8,128)} copy(s32[128,8]{0,1:T(8,128)} %param.9) | data formatting | bytes 8192 | tf_op args[2]
  2.7 1.4 %copy.9.factor_ref = f32[128,8]{1,0:T(8,128)} copy(f32[128,8]{0,1:T(8,128)} %param.10) | data formatting | bytes 8192 | tf_op args[3]
  4.1 71.0 %shard_map.73 = bf16[128,512]{1,0:T(8,128)(2,1)} custom-call(bf16[128,512]{1,0:T(8,128)(2,1)} %tokens_ref.1, bf16[1,2048]{1,0:T(2,128)(2,1)} %reshape.3.gain_ref, s32[128,8]{1,0:T(8,128)} %copy.8.ids_ref, f32[128,8]{1,0:T(8,128)} %copy.9.factor_ref, bf16[16,384,2048]{2,1,0:T(8,128)(2,1)} %gate_hbm.1, bf16[16,384,2048]{2,1,0:T(8,128)(2,1)} %up_hbm.1, ...), custom_call_target="tpu_custom_call" | custom-call | flops 9663676416 | bytes 75497472 | tf_op jit(solution)/shard_map/pallas_call | solution.py:367
  75.2 1.6 %copy.11 = bf16[128,512]{1,0:T(8,128)(2,1)} copy(bf16[128,512]{1,0:T(8,128)(2,1)} %shard_map.73) | data formatting | bytes 262144
